TPU v7x, 128 devices: a whole 4x4x4 slice. The times are simulated.
128 devices in a mesh: col: 8 (over z, core), row: 16 (over x, y).
Axes of the slice: x: 4, y: 4, z: 4, core: 2. Of those that a mesh axis runs over, the one named last changes fastest.
Arguments:
- affinity: bfloat16 [15360, 128, 128], P(('col', 'row')), may hold values from 0 to 0.015625
- tile_rows: int32 [15360], P(('col', 'row')), may hold values from 0 to 39
- tile_cols: int32 [15360], P(('col', 'row')), may hold values from 0 to 79
- live_tiles: int32 [128], P(('col', 'row')), may hold values from 1 to 120, as said below
- start: float32 [81920, 256], P(('col', 'row')), may hold values from -1500 to 1500
Outputs:
- vectors: float32 [81920, 256], P(('col', 'row'))
- first_passes: float32 [2, 81920, 256], P(None, ('col', 'row'))
Inputs may be any that keep to these rules, and one draw needn't show every extreme that they name: A device's tiles are its slots 0 to live_tiles - 1; later slots are ignored. Some device holds exactly 120 tiles.
All inputs are finite; a program needn't handle non-finite values.
Results may differ from a plain program's by a relative error of at most 0.0003.
Values sent between devices are 32-bit elements; how exact they have to be, the bound alone decides.
A program may use at most 128 MiB of HBM per device.

v0:
```python
import jax
import jax.numpy as jnp
from jax import lax
from jax.sharding import Mesh
from jax.sharding import PartitionSpec as P

ITERS = 2
ROW = ("row_0", "row_1")
COL = ("col_0", "col_1")
COL_ROW = ("col_0", "col_1", "row_0", "row_1")
highest = lax.Precision.HIGHEST


def cut_along(value, dim, devices):
    before, after = (value.shape[:dim], value.shape[dim + 1 :])
    return jnp.moveaxis(value.reshape(*before, devices, -1, *after), dim, 0)


def sent_and_summed(value, axis, dim):
    parts = cut_along(value, dim, lax.axis_size(axis))
    arrived = lax.all_to_all(parts, axis, split_axis=0, concat_axis=0, tiled=True)
    return arrived.sum(axis=0)


def sum_in_two_steps(value, axes, dim):
    far, near = axes
    parts = cut_along(value, dim, lax.axis_size(far))
    nearer = sent_and_summed(parts, near, dim + 1)
    arrived = lax.all_to_all(nearer, far, split_axis=0, concat_axis=0, tiled=True)
    return arrived.sum(axis=0)


def rows_for(lines, devices):
    spare = -lines.shape[0] % devices
    if not spare:
        return lines
    return jnp.concatenate([lines, jnp.zeros((spare, *lines.shape[1:]), lines.dtype)])


def sent_to_all(value, axis):
    copies = jnp.broadcast_to(value, (lax.axis_size(axis), *value.shape))
    return lax.all_to_all(copies, axis, split_axis=0, concat_axis=0, tiled=True)


def joined_along(parts, dim):
    lengths = list(parts.shape[1:])
    lengths[dim] *= parts.shape[0]
    return jnp.moveaxis(parts, 0, dim).reshape(lengths)


def whole_of(value, axes, dim):
    far, near = axes
    initial = sent_to_all(value, far)
    parts = jnp.swapaxes(sent_to_all(initial, near), 0, 1)
    return joined_along(parts.reshape(-1, *value.shape), dim)


def nested_sum(value, axes):
    lines = value.reshape(-1, value.shape[-1])
    own = sum_in_two_steps(
        rows_for(lines, lax.axis_size(axes[0]) * lax.axis_size(axes[1])), axes, 0
    )
    whole = whole_of(own, axes, 0)
    return whole[: len(lines)].reshape(value.shape)


def total_of(value, axes):
    own = sum_in_two_steps(
        rows_for(value, lax.axis_size(axes[0]) * lax.axis_size(axes[1])), axes, 0
    )
    whole = whole_of(own, axes, 0)
    return whole[: len(value)].reshape(value.shape)


def together(arrays, axis):
    ends = [0]
    for a in arrays:
        ends.append(ends[-1] + a.size)
    subtotal = total_of(jnp.concatenate([a.ravel() for a in arrays]), axis)
    return tuple((subtotal[b:e].reshape(a.shape) for a, b, e in zip(arrays, ends, ends[1:])))


def local_gram(matrix):
    return jnp.dot(matrix.T, matrix, precision=highest, preferred_element_type=jnp.float32)


def inverse_lower(gram):
    lower = jnp.linalg.cholesky(gram)
    return jax.scipy.linalg.solve_triangular(
        lower, jnp.eye(gram.shape[0], dtype=jnp.float32), lower=True
    )


def apply_factor(matrix, inverse):
    return jnp.dot(matrix, inverse.T, precision=highest, preferred_element_type=jnp.float32)


def body(affinity, tile_rows, tile_cols, live_tiles, start):
    n_row = lax.axis_size(ROW)
    n_col = lax.axis_size(COL)
    slot_count = affinity.shape[0]
    tile_size = affinity.shape[1]
    rows_local = start.shape[0]
    vec_count = start.shape[1]
    own_tiles = rows_local // tile_size
    live = (jnp.arange(slot_count) < live_tiles[0]).astype(jnp.float32)
    row_onehot = (jnp.arange(own_tiles * n_col)[:, None] == tile_rows[None, :]).astype(
        jnp.float32
    ) * live[None, :]
    row_sums = jnp.sum(affinity, axis=2, dtype=jnp.float32)
    degree_terms = jnp.dot(
        row_onehot, row_sums, precision=highest, preferred_element_type=jnp.float32
    )
    degree = 1.0 + sent_and_summed(degree_terms, COL, 0).reshape(rows_local)
    scaling = (1.0 / jnp.sqrt(degree))[:, None]
    squares = affinity.astype(jnp.float32)
    firsts = []
    pending = start
    for step_number in range(ITERS):
        mapped_scaled = scaling * pending
        gathered = lax.all_gather(mapped_scaled, ROW, axis=0, tiled=True)
        gathered = gathered.reshape(n_row * own_tiles, tile_size, vec_count)
        picked = gathered[tile_cols]
        products = jnp.einsum(
            "sij,sjk->sik", squares, picked, precision=highest, preferred_element_type=jnp.float32
        )
        terms = jnp.dot(
            row_onehot,
            products.reshape(slot_count, tile_size * vec_count),
            precision=highest,
            preferred_element_type=jnp.float32,
        )
        summed = sum_in_two_steps(terms, ("col_0", "col_1"), 0)
        raw_image = scaling * (mapped_scaled + summed.reshape(rows_local, vec_count))
        if step_number == 0:
            inner_gram = nested_sum(local_gram(raw_image), (("col_0", "col_1", "row_0"), "row_1"))
            image_block = raw_image
        else:
            raw_gram, pending_gram = together(
                (local_gram(raw_image), local_gram(pending)), (("col_0", "col_1", "row_0"), "row_1")
            )
            pending_inverse = inverse_lower(pending_gram)
            image_block = apply_factor(raw_image, pending_inverse)
            inner_gram = jnp.dot(
                jnp.dot(
                    pending_inverse, raw_gram, precision=highest, preferred_element_type=jnp.float32
                ),
                pending_inverse.T,
                precision=highest,
                preferred_element_type=jnp.float32,
            )
        pending = apply_factor(image_block, inverse_lower(inner_gram))
        firsts.append(pending)
    final_gram = nested_sum(local_gram(pending), (("col_0", "col_1", "row_0"), "row_1"))
    basis = apply_factor(pending, inverse_lower(final_gram))
    total_images = rows_local * n_row * n_col
    root = jnp.sqrt(jnp.float32(total_images))
    return (root * basis, root * jnp.stack(firsts, axis=0))


def solution(mesh):
    torus = Mesh(mesh.devices.reshape(4, 2, 4, 4), ("col_0", "col_1", "row_0", "row_1"))
    return jax.shard_map(
        body,
        mesh=torus,
        in_specs=(P(COL_ROW, None, None), P(COL_ROW), P(COL_ROW), P(COL_ROW), P(COL_ROW, None)),
        out_specs=(P(COL_ROW, None), P(None, COL_ROW, None)),
        check_vma=False,
    )
```

profile of v0, /device:TPU:0, one launch (start us, length us, event | category | flops | bytes accessed | tf_op | source)
XLA Modules:
  0.0 914.5 jit_solution(9744506423480880370)
XLA Ops:
  12.6 5.4 all-to-all-start
  18.1 5.4 all-to-all-done
  26.3 79.2 %all-gather.3.cloned.1.call-done = f32[10240,256]{1,0:T(8,128)} async-done(((f32[640,256]{1,0:T(8,128)}), f32[10240,256]{1,0:T(8,128)}) %all-gather.3.cloned.1.call-update) | async-done | bytes 10485776 | tf_op jit(solution)/shard_map/all_gather | solution.py:121
  105.5 13.6 %gather_fusion = f32[120,128,256]{2,1,0:T(8,128)} fusion(f32[80,128,256]{2,1,0:T(8,128)} %bitcast.176, s32[1024]{0:T(1024)S(1)} %pad_clamp_fusion), kind=kCustom, calls=%fused_computation | custom fusion | bytes 31457760 | tf_op jit(solution)/shard_map/gather | solution.py:123
  119.1 20.2 %convolution_bitcast_fusion.3 = f32[120,128,256]{1,2,0:T(8,128)} fusion(f32[120,128,256]{2,1,0:T(8,128)} %gather_fusion, bf16[120,128,128]{2,1,0:T(8,128)(2,1)} %param.8), kind=kOutput, calls=%fused_computation.15 | convolution fusion | flops 6039797760 | bytes 35389440 | tf_op jit(solution)/shard_map/sij,sjk->sik/dot_general | solution.py:124
  139.3 15.6 %copy.101 = f32[120,128,256]{2,1,0:T(8,128)} copy(f32[120,128,256]{1,2,0:T(8,128)} %convolution_bitcast_fusion.3) | data formatting | bytes 31457280 | tf_op jit(solution)/shard_map/sij,sjk->sik/dot_general | solution.py:124
  154.9 17.9 %reshape.193 = f32[120,32768,1,1]{1,0,2,3:T(8,128)} reshape(f32[120,128,256]{2,1,0:T(8,128)} %copy.101) | data formatting | bytes 31457280 | tf_op jit(solution)/shard_map/reshape | solution.py:129
  172.8 16.1 %convolution_bitcast_fusion.1 = f32[2,4,5,32768]{3,2,0,1:T(8,128)S(1)} fusion(f32[120,32768,1,1]{1,0,2,3:T(8,128)} %reshape.193, f32[120]{0:T(128)S(1)} %compare_convert_fusion, s32[120]{0:T(128)S(1)} %copy-done.1, s32[4,2,5]{2,1,0:T(2,128)S(1)} %multiply_add_fusion), kind=kOutput, calls=%fused_computation.11 | convolution fusion | flops 1887446400 | bytes 20972640 | tf_op jit(solution)/shard_map/dot_general | solution.py:127
  192.3 9.1 all_to_all.93
  207.5 63.5 %all_to_all.97 = f32[4,5,32768]{2,1,0:T(8,128)} all-to-all(f32[4,5,32768]{2,1,0:T(8,128)S(1)} %copy.103), channel_id=1, replica_groups=mesh['col_0'=4,'col_1'=2,'row_0'=4,'row_1'=4] {'col_0'}, dimensions={0} | all-to-all | bytes 5242880 | tf_op jit(solution)/shard_map/all_to_all | solution.py:29
  275.5 10.7 %all_to_all.98 = f32[4,32,2,256]{3,2,1,0:T(2,128)S(1)} all-to-all(f32[4,32,2,256]{3,2,1,0:T(2,128)S(1)} %bitcast.182), channel_id=1, replica_groups=mesh['col_0'=4,'col_1'=2,'row_0'=4,'row_1'=4] {'row_1'}, dimensions={0} | all-to-all | bytes 524288 | tf_op jit(solution)/shard_map/all_to_all | solution.py:21
  286.3 11.0 %all_to_all.99 = f32[32,2,256]{2,1,0:T(2,128)S(1)} all-to-all(f32[32,2,256]{2,1,0:T(2,128)S(1)} %reduce_sum.112), channel_id=1, replica_groups=mesh['col_0'=4,'col_1'=2,'row_0'=4,'row_1'=4] {'col_0','col_1','row_0'}, dimensions={0} | all-to-all | bytes 131072 | tf_op jit(solution)/shard_map/all_to_all | solution.py:29
  301.9 7.4 all-to-all-done.5
  313.6 7.1 all-to-all-done.6
  321.1 11.7 %cholesky.214 = f32[128,128]{1,0:T(8,128)S(1)} custom-call(f32[128,128]{1,0:T(8,128)S(1)} %cholesky.346), custom_call_target="Cholesky" | custom-call | tf_op jit(solution)/shard_map/jit(cholesky)/cholesky | solution.py:88
  332.9 9.8 %custom-call.17 = f32[1,128,128]{1,2,0:T(8,128)S(1)} custom-call(f32[1,128,128]{2,1,0:T(8,128)S(1)} %get-tuple-element.91), custom_call_target="InvertDiagBlocksLowerTriangular" | custom-call | tf_op jit(solution)/shard_map/jit(cholesky)/cholesky | solution.py:88
  343.2 11.7 %cholesky.231 = f32[128,128]{1,0:T(8,128)S(1)} custom-call(f32[128,128]{1,0:T(8,128)S(1)} %convolution_subtract_fusion.7), custom_call_target="Cholesky" | custom-call | tf_op jit(solution)/shard_map/jit(cholesky)/cholesky | solution.py:88
  357.1 4.5 while.8
  362.2 19.7 %custom-call.18 = f32[2,128,128]{1,2,0:T(8,128)S(1)} custom-call(f32[2,128,128]{2,1,0:T(8,128)S(1)} %get-tuple-element.30), custom_call_target="InvertDiagBlocksLowerTriangular" | custom-call | tf_op jit(solution)/shard_map/jit(_solve_triangular)/triangular_solve | solution.py:89
  384.4 75.9 %all-gather.5.cloned.1.call-done = f32[10240,256]{1,0:T(8,128)} async-done(((f32[640,256]{1,0:T(8,128)}), f32[10240,256]{1,0:T(8,128)}) %all-gather.5.cloned.1.call-update) | async-done | bytes 10485776 | tf_op jit(solution)/shard_map/all_gather | solution.py:121
  460.3 13.6 %gather_fusion.1 = f32[120,128,256]{2,1,0:T(8,128)} fusion(f32[80,128,256]{2,1,0:T(8,128)} %bitcast.177, s32[1024]{0:T(1024)S(1)} %pad_clamp_fusion), kind=kCustom, calls=%fused_computation.1 | custom fusion | bytes 31457760 | tf_op jit(solution)/shard_map/gather | solution.py:123
  473.9 20.2 %convolution_bitcast_fusion.2 = f32[120,128,256]{1,2,0:T(8,128)} fusion(f32[120,128,256]{2,1,0:T(8,128)} %gather_fusion.1, bf16[120,128,128]{2,1,0:T(8,128)(2,1)} %param.8), kind=kOutput, calls=%fused_computation.14 | convolution fusion | flops 6039797760 | bytes 35389440 | tf_op jit(solution)/shard_map/sij,sjk->sik/dot_general | solution.py:124
  494.1 15.6 %copy.109 = f32[120,128,256]{2,1,0:T(8,128)} copy(f32[120,128,256]{1,2,0:T(8,128)} %convolution_bitcast_fusion.2) | data formatting | bytes 31457280 | tf_op jit(solution)/shard_map/sij,sjk->sik/dot_general | solution.py:124
  509.7 17.9 %reshape.194 = f32[120,32768,1,1]{1,0,2,3:T(8,128)} reshape(f32[120,128,256]{2,1,0:T(8,128)} %copy.109) | data formatting | bytes 31457280 | tf_op jit(solution)/shard_map/reshape | solution.py:129
  527.5 16.0 %convolution_bitcast_fusion = f32[2,4,5,32768]{3,2,0,1:T(8,128)S(1)} fusion(f32[120,32768,1,1]{1,0,2,3:T(8,128)} %reshape.194, f32[120]{0:T(128)S(1)} %copy-done.3, s32[120]{0:T(128)S(1)} %copy-done.1, s32[4,2,5]{2,1,0:T(2,128)S(1)} %multiply_add_fusion), kind=kOutput, calls=%fused_computation.10 | convolution fusion | flops 1887446400 | bytes 20972640 | tf_op jit(solution)/shard_map/dot_general | solution.py:127
  547.0 9.1 all_to_all.94
  564.1 4.9 all-to-all-start.8
  570.5 47.9 %all-to-all-done.8 = f32[4,5,32768]{2,1,0:T(8,128)} async-done(((f32[4,5,32768]{2,1,0:T(8,128)}), f32[4,5,32768]{2,1,0:T(8,128)}, u32[]{:S(2)}, u32[]{:S(2)}) %all-to-all-start.8) | async-done | bytes 2621472 | tf_op jit(solution)/shard_map/all_to_all | solution.py:29
  623.1 13.0 %all_to_all.100 = f32[4,32,1024]{2,1,0:T(8,128)S(1)} all-to-all(f32[4,32,1024]{2,1,0:T(8,128)S(1)} %maximum_bitcast_fusion), channel_id=1, replica_groups=mesh['col_0'=4,'col_1'=2,'row_0'=4,'row_1'=4] {'row_1'}, dimensions={0} | all-to-all | bytes 1048576 | tf_op jit(solution)/shard_map/all_to_all | solution.py:21
  636.2 11.7 %all_to_all.101 = f32[32,1,1024]{2,1,0:T(1,128)S(1)} all-to-all(f32[32,1,1024]{2,1,0:T(1,128)S(1)} %all_to_all.67), channel_id=1, replica_groups=mesh['col_0'=4,'col_1'=2,'row_0'=4,'row_1'=4] {'col_0','col_1','row_0'}, dimensions={0} | all-to-all | bytes 262144 | tf_op jit(solution)/shard_map/all_to_all | solution.py:29
  648.1 11.5 %all_to_all.95 = f32[32,1,1024]{2,1,0:T(1,128)S(1)} all-to-all(f32[32,1,1024]{2,1,0:T(1,128)S(1)} %broadcast_in_dim.30), channel_id=1, replica_groups=mesh['col_0'=4,'col_1'=2,'row_0'=4,'row_1'=4] {'col_0','col_1','row_0'}, dimensions={0} | all-to-all | bytes 262144 | tf_op jit(solution)/shard_map/all_to_all | solution.py:42
  663.9 10.1 %all-to-all-done.12 = f32[4,32,1024]{2,1,0:T(8,128)S(1)} async-done(((f32[4,32,1024]{2,1,0:T(8,128)}), f32[4,32,1024]{2,1,0:T(8,128)S(1)}, u32[]{:S(2)}, u32[]{:S(2)}) %all-to-all-start.12) | async-done | bytes 524320 | tf_op jit(solution)/shard_map/all_to_all | solution.py:42
  674.6 11.7 %cholesky.248 = f32[128,128]{1,0:T(8,128)S(1)} custom-call(f32[128,128]{1,0:T(8,128)S(1)} %cholesky.349), custom_call_target="Cholesky" | custom-call | tf_op jit(solution)/shard_map/jit(cholesky)/cholesky | solution.py:88
  686.4 9.8 %custom-call.19 = f32[1,128,128]{1,2,0:T(8,128)S(1)} custom-call(f32[1,128,128]{2,1,0:T(8,128)S(1)} %get-tuple-element.87), custom_call_target="InvertDiagBlocksLowerTriangular" | custom-call | tf_op jit(solution)/shard_map/jit(cholesky)/cholesky | solution.py:88
  696.7 11.7 %cholesky.265 = f32[128,128]{1,0:T(8,128)S(1)} custom-call(f32[128,128]{1,0:T(8,128)S(1)} %convolution_subtract_fusion.6), custom_call_target="Cholesky" | custom-call | tf_op jit(solution)/shard_map/jit(cholesky)/cholesky | solution.py:88
  715.1 19.8 %custom-call.20 = f32[2,128,128]{1,2,0:T(8,128)S(1)} custom-call(f32[2,128,128]{2,1,0:T(8,128)S(1)} %get-tuple-element.31), custom_call_target="InvertDiagBlocksLowerTriangular" | custom-call | tf_op jit(solution)/shard_map/jit(_solve_triangular)/triangular_solve | solution.py:89
  737.9 11.7 %cholesky.282 = f32[128,128]{1,0:T(8,128)S(1)} custom-call(f32[128,128]{1,0:T(8,128)S(1)} %cholesky.352), custom_call_target="Cholesky" | custom-call | tf_op jit(solution)/shard_map/jit(cholesky)/cholesky | solution.py:88
  749.7 9.8 %custom-call.21 = f32[1,128,128]{1,2,0:T(8,128)S(1)} custom-call(f32[1,128,128]{2,1,0:T(8,128)S(1)} %get-tuple-element.83), custom_call_target="InvertDiagBlocksLowerTriangular" | custom-call | tf_op jit(solution)/shard_map/jit(cholesky)/cholesky | solution.py:88
  760.0 11.9 %cholesky.299 = f32[128,128]{1,0:T(8,128)S(1)} custom-call(f32[128,128]{1,0:T(8,128)S(1)} %convolution_subtract_fusion.5), custom_call_target="Cholesky" | custom-call | tf_op jit(solution)/shard_map/jit(cholesky)/cholesky | solution.py:88
  778.6 19.7 %custom-call.22 = f32[2,128,128]{1,2,0:T(8,128)S(1)} custom-call(f32[2,128,128]{2,1,0:T(8,128)S(1)} %get-tuple-element.32), custom_call_target="InvertDiagBlocksLowerTriangular" | custom-call | tf_op jit(solution)/shard_map/jit(_solve_triangular)/triangular_solve | solution.py:89
  801.3 9.1 all_to_all.102
  810.5 10.5 %all_to_all.103 = f32[32,2,256]{2,1,0:T(2,128)S(1)} all-to-all(f32[32,2,256]{2,1,0:T(2,128)S(1)} %reduce_sum.118), channel_id=1, replica_groups=mesh['col_0'=4,'col_1'=2,'row_0'=4,'row_1'=4] {'col_0','col_1','row_0'}, dimensions={0} | all-to-all | bytes 131072 | tf_op jit(solution)/shard_map/all_to_all | solution.py:29
  821.0 11.0 %all_to_all.96 = f32[32,2,256]{2,1,0:T(2,128)S(1)} all-to-all(f32[32,2,256]{2,1,0:T(2,128)S(1)} %broadcast_in_dim.32), channel_id=1, replica_groups=mesh['col_0'=4,'col_1'=2,'row_0'=4,'row_1'=4] {'col_0','col_1','row_0'}, dimensions={0} | all-to-all | bytes 131072 | tf_op jit(solution)/shard_map/all_to_all | solution.py:42
  837.6 6.0 all-to-all-done.16
  844.0 11.7 %cholesky.316 = f32[128,128]{1,0:T(8,128)S(1)} custom-call(f32[128,128]{1,0:T(8,128)S(1)} %cholesky.355), custom_call_target="Cholesky" | custom-call | tf_op jit(solution)/shard_map/jit(cholesky)/cholesky | solution.py:88
  855.8 9.8 %custom-call.23 = f32[1,128,128]{1,2,0:T(8,128)S(1)} custom-call(f32[1,128,128]{2,1,0:T(8,128)S(1)} %get-tuple-element.79), custom_call_target="InvertDiagBlocksLowerTriangular" | custom-call | tf_op jit(solution)/shard_map/jit(cholesky)/cholesky | solution.py:88
  866.1 11.7 %cholesky.333 = f32[128,128]{1,0:T(8,128)S(1)} custom-call(f32[128,128]{1,0:T(8,128)S(1)} %convolution_subtract_fusion.4), custom_call_target="Cholesky" | custom-call | tf_op jit(solution)/shard_map/jit(cholesky)/cholesky | solution.py:88
  884.7 20.0 %custom-call.24 = f32[2,128,128]{1,2,0:T(8,128)S(1)} custom-call(f32[2,128,128]{2,1,0:T(8,128)S(1)} %get-tuple-element.33), custom_call_target="InvertDiagBlocksLowerTriangular" | custom-call | tf_op jit(solution)/shard_map/jit(_solve_triangular)/triangular_solve | solution.py:89
  (173 shorter events, 106.5 us)
Async XLA Ops:
  7.8 165.0 %copy-start.2 = (f32[120]{0:T(128)}, f32[120]{0:T(128)S(1)}, u32[]{:S(2)}) copy-start(f32[120]{0:T(128)S(1)} %compare_convert_fusion) | copy-start | bytes 1444
  12.6 10.8 %all-to-all-start = ((f32[8,5,128]{2,1,0:T(8,128)}), f32[8,5,128]{2,1,0:T(8,128)S(1)}, u32[]{:S(2)}, u32[]{:S(2)}) async-start(f32[8,5,128]{2,1,0:T(8,128)} %fusion.51), calls=%async_computation | async-start | bytes 65536 | tf_op jit(solution)/shard_map/all_to_all | solution.py:21
  18.0 87.5 %all-gather.3.cloned.1.call-start = ((), (), s32[]{:S(2)}) async-start(), calls=%async_computation.17 | async-start | bytes 11141120 | tf_op jit(solution)/shard_map/all_gather | solution.py:121
  154.9 17.9 %copy-start.1 = (s32[120]{0:T(128)S(1)}, s32[120]{0:T(128)}, u32[]{:S(2)}) copy-start(s32[120]{0:T(128)} %param.9) | copy-start | bytes 1444
  205.8 68.0 %copy-start = (f32[640,256]{1,0:T(8,128)S(1)}, f32[640,256]{1,0:T(8,128)}, u32[]{:S(2)}) copy-start(f32[640,256]{1,0:T(8,128)} %param.12) | copy-start | bytes 1966084
  298.0 11.3 %all-to-all-start.5 = ((f32[32,2,256]{2,1,0:T(2,128)}), f32[32,2,256]{2,1,0:T(2,128)S(1)}, u32[]{:S(2)}, u32[]{:S(2)}) async-start(f32[32,2,256]{2,1,0:T(2,128)} %broadcast_in_dim.28), calls=%async_computation.5 | async-start | bytes 131072 | tf_op jit(solution)/shard_map/all_to_all | solution.py:42
  310.1 10.6 %all-to-all-start.6 = ((f32[4,32,2,256]{3,2,1,0:T(2,128)}), f32[4,32,2,256]{3,2,1,0:T(2,128)S(1)}, u32[]{:S(2)}, u32[]{:S(2)}) async-start(f32[4,32,2,256]{3,2,1,0:T(2,128)} %broadcast_in_dim.29), calls=%async_computation.6 | async-start | bytes 524288 | tf_op jit(solution)/shard_map/all_to_all | solution.py:42
  313.5 146.8 %all-gather.5.cloned.1.call-start = ((), (), s32[]{:S(2)}) async-start(), calls=%async_computation.18 | async-start | bytes 11141120 | tf_op jit(solution)/shard_map/all_gather | solution.py:121
  361.7 0.6 copy-start.4
  509.7 17.9 %copy-start.3 = (f32[120]{0:T(128)S(1)}, f32[120]{0:T(128)}, u32[]{:S(2)}) copy-start(f32[120]{0:T(128)} %copy-done.2) | copy-start | bytes 1444
  564.1 54.3 %all-to-all-start.8 = ((f32[4,5,32768]{2,1,0:T(8,128)}), f32[4,5,32768]{2,1,0:T(8,128)}, u32[]{:S(2)}, u32[]{:S(2)}) async-start(f32[4,5,32768]{2,1,0:T(8,128)} %copy.111), calls=%async_computation.8 | async-start | bytes 8388608 | tf_op jit(solution)/shard_map/all_to_all | solution.py:29
  570.3 140.7 %copy-start.5 = (s32[2,2]{1,0:T(2,128)S(1)}, s32[2,2]{1,0:T(2,128)}, u32[]{:S(2)}) copy-start(s32[2,2]{1,0:T(2,128)} %copy-done.4) | copy-start | bytes 52
  660.4 13.6 %all-to-all-start.12 = ((f32[4,32,1024]{2,1,0:T(8,128)}), f32[4,32,1024]{2,1,0:T(8,128)S(1)}, u32[]{:S(2)}, u32[]{:S(2)}) async-start(f32[4,32,1024]{2,1,0:T(8,128)} %broadcast_in_dim.31), calls=%async_computation.12 | async-start | bytes 1048576 | tf_op jit(solution)/shard_map/all_to_all | solution.py:42
  832.8 10.8 %all-to-all-start.16 = ((f32[4,32,2,256]{3,2,1,0:T(2,128)}), f32[4,32,2,256]{3,2,1,0:T(2,128)S(1)}, u32[]{:S(2)}, u32[]{:S(2)}) async-start(f32[4,32,2,256]{3,2,1,0:T(2,128)} %broadcast_in_dim.33), calls=%async_computation.16 | async-start | bytes 524288 | tf_op jit(solution)/shard_map/all_to_all | solution.py:42
Sparse Core Ops, SparseCore 0:
  25.7 79.7 all-gather.2
  384.5 75.7 all-gather.4
where the time goes:
time: 925 us; the launch traced here: 915 us
  other arithmetic  240 us (26%)
  waiting for transfers between devices  239 us (26%)
  blocking collectives  170 us (18%)
  local copies, waits for them, and re-layouts  130 us (14%)
  matrix products  89.4 us (10%)
  starting transfers between devices  24.7 us (3%)
  between operations  21.3 us (2%)
    all_gather x2, waiting for transfers between devices, body(): gathered = lax.all_gather(mapped_scaled, ROW, axis=0, tiled=True)  155 us
    another operation x27, other arithmetic, inverse_lower(): lower = jnp.linalg.cholesky(gram)  138 us
    all_to_all x4, blocking collectives, sum_in_two_steps(): lax.all_to_all(nearer, far, split_axis=0, concat_axis=0, tiled=True)  96.7 us
    another operation x9, other arithmetic, inverse_lower(): jax.scipy.linalg.solve_triangular(lower, jnp.eye(gram.shape[0], dtype=jnp...  79.3 us
    all_to_all x5, blocking collectives, sent_and_summed(): lax.all_to_all(parts, axis, split_axis=0, concat_axis=0, tiled=True)  50.9 us
    all_to_all x1, waiting for transfers between devices, sum_in_two_steps(): lax.all_to_all(nearer, far, split_axis=0, concat_axis=0, tiled=True)  47.9 us
    dot_general x2, matrix products, body(): jnp.einsum('sij,sjk->sik', squares, picked, precision=highest, preferred_...  40.3 us
    reshape x2, local copies, waits for them, and re-layouts, body(): products.reshape(slot_count, tile_size * vec_count)  35.7 us
  transfers between devices with their start and end apart: 8, of which 8 were waited for; matrix products, arithmetic and copies ran while one was open for 0% of the time, Pallas kernels for 0%

commit v1 on v0

--- a/solution.py
+++ b/solution.py
@@ -118,7 +118,19 @@
     pending = start
     for step_number in range(ITERS):
         mapped_scaled = scaling * pending
-        gathered = lax.all_gather(mapped_scaled, ROW, axis=0, tiled=True)
+
+        def review_sums_all(block_in):
+            return jnp.concatenate(
+                jax.lax.all_to_all(
+                    jnp.stack([block_in for _ in range(jax.lax.axis_size(ROW))], 0),
+                    axis_name=ROW,
+                    split_axis=0,
+                    concat_axis=0,
+                ),
+                0,
+            )
+
+        gathered = review_sums_all(mapped_scaled)
         gathered = gathered.reshape(n_row * own_tiles, tile_size, vec_count)
         picked = gathered[tile_cols]
         products = jnp.einsum(

time: 925 us -> 1070 us (1.16)
  blocking collectives: 170 us -> 297 us
  waiting for transfers between devices: 239 us -> 266 us
  between operations: 21.3 us -> 7.95 us
    all_to_all x0 -> x1, waiting for transfers between devices: none -> 182 us  [review_sums_all(): jax.lax.all_to_all(jnp.stack([block_in for _ in range(jax.lax.axis_size(R...]
    all_gather x2 -> x0, waiting for transfers between devices: 155 us -> none  [body(): gathered = lax.all_gather(mapped_scaled, ROW, axis=0, tiled=True)]
    all_to_all x0 -> x1, blocking collectives: none -> 121 us  [review_sums_all(): jax.lax.all_to_all(jnp.stack([block_in for _ in range(jax.lax.axis_size(R...]
  transfers between devices with their start and end apart: 8 -> 7, of which waited for: 8 -> 7; matrix products, arithmetic and copies ran while one was open for 0% -> 0% of each run, Pallas kernels for 0% -> 0%
where the time goes in v1:
time: 1070 us
  blocking collectives  297 us (28%)
  waiting for transfers between devices  266 us (25%)
  other arithmetic  239 us (22%)
  local copies, waits for them, and re-layouts  136 us (13%)
  matrix products  88.6 us (8%)
  starting transfers between devices  32.5 us (3%)
    all_to_all x1, waiting for transfers between devices, review_sums_all(): jax.lax.all_to_all(jnp.stack([block_in for _ in range(jax.lax.axis_size(R...  182 us
    another operation x27, other arithmetic, inverse_lower(): lower = jnp.linalg.cholesky(gram)  138 us
    all_to_all x1, blocking collectives, review_sums_all(): jax.lax.all_to_all(jnp.stack([block_in for _ in range(jax.lax.axis_size(R...  121 us
    all_to_all x4, blocking collectives, sum_in_two_steps(): lax.all_to_all(nearer, far, split_axis=0, concat_axis=0, tiled=True)  102 us
    another operation x9, other arithmetic, inverse_lower(): jax.scipy.linalg.solve_triangular(lower, jnp.eye(gram.shape[0], dtype=jnp...  79.7 us
    all_to_all x5, blocking collectives, sent_and_summed(): lax.all_to_all(parts, axis, split_axis=0, concat_axis=0, tiled=True)  51.8 us
    all_to_all x1, waiting for transfers between devices, sum_in_two_steps(): lax.all_to_all(nearer, far, split_axis=0, concat_axis=0, tiled=True)  47.9 us
    dot_general x2, matrix products, body(): jnp.einsum('sij,sjk->sik', squares, picked, precision=highest, preferred_...  40.3 us
  transfers between devices with their start and end apart: 7, of which 7 were waited for; matrix products, arithmetic and copies ran while one was open for 0% of the time, Pallas kernels for 0%

profile of v1, /device:TPU:0, one launch (start us, length us, event | category | flops | bytes accessed | tf_op | source)
XLA Modules:
  0.0 1067.2 jit_solution(8905205009067602785)
XLA Ops:
  6.1 5.4 all-to-all-start
  11.5 5.4 all-to-all-done
  23.2 7.4 all-to-all-start.1
  30.7 182.3 %all-to-all-done.1 = f32[16,640,256]{2,1,0:T(8,128)} async-done(((f32[16,640,256]{2,1,0:T(8,128)}), f32[16,640,256]{2,1,0:T(8,128)}, u32[]{:S(2)}, u32[]{:S(2)}) %all-to-all-start.1) | async-done | bytes 10485792 | tf_op jit(solution)/shard_map/all_to_all | solution.py:124
  213.0 13.6 %gather_fusion = f32[120,128,256]{2,1,0:T(8,128)} fusion(f32[80,128,256]{2,1,0:T(8,128)} %bitcast.3, s32[1024]{0:T(1024)S(1)} %pad_clamp_fusion), kind=kCustom, calls=%fused_computation | custom fusion | bytes 31457760 | tf_op jit(solution)/shard_map/gather | solution.py:135
  226.6 20.2 %convolution_bitcast_fusion.3 = f32[120,128,256]{1,2,0:T(8,128)} fusion(f32[120,128,256]{2,1,0:T(8,128)} %gather_fusion, bf16[120,128,128]{2,1,0:T(8,128)(2,1)} %param.8), kind=kOutput, calls=%fused_computation.15 | convolution fusion | flops 6039797760 | bytes 35389440 | tf_op jit(solution)/shard_map/sij,sjk->sik/dot_general | solution.py:136
  246.8 15.6 %copy.101 = f32[120,128,256]{2,1,0:T(8,128)} copy(f32[120,128,256]{1,2,0:T(8,128)} %convolution_bitcast_fusion.3) | data formatting | bytes 31457280 | tf_op jit(solution)/shard_map/sij,sjk->sik/dot_general | solution.py:136
  262.4 17.9 %reshape.189 = f32[120,32768,1,1]{1,0,2,3:T(8,128)} reshape(f32[120,128,256]{2,1,0:T(8,128)} %copy.101) | data formatting | bytes 31457280 | tf_op jit(solution)/shard_map/reshape | solution.py:141
  280.3 16.2 %convolution_bitcast_fusion.1 = f32[2,4,5,32768]{3,2,0,1:T(8,128)S(1)} fusion(f32[120,32768,1,1]{1,0,2,3:T(8,128)} %reshape.189, f32[120]{0:T(128)S(1)} %compare_convert_fusion, s32[120]{0:T(128)S(1)} %copy-done.1, s32[4,2,5]{2,1,0:T(2,128)S(1)} %multiply_add_fusion), kind=kOutput, calls=%fused_computation.11 | convolution fusion | flops 1887446400 | bytes 20972640 | tf_op jit(solution)/shard_map/dot_general | solution.py:139
  299.8 9.1 all_to_all.103
  315.0 62.9 %all_to_all.107 = f32[4,5,32768]{2,1,0:T(8,128)} all-to-all(f32[4,5,32768]{2,1,0:T(8,128)S(1)} %copy.103), channel_id=1, replica_groups=mesh['col_0'=4,'col_1'=2,'row_0'=4,'row_1'=4] {'col_0'}, dimensions={0} | all-to-all | bytes 5242880 | tf_op jit(solution)/shard_map/all_to_all | solution.py:29
  382.5 12.9 %all_to_all.108 = f32[4,32,2,256]{3,2,1,0:T(2,128)S(1)} all-to-all(f32[4,32,2,256]{3,2,1,0:T(2,128)S(1)} %bitcast.181), channel_id=1, replica_groups=mesh['col_0'=4,'col_1'=2,'row_0'=4,'row_1'=4] {'row_1'}, dimensions={0} | all-to-all | bytes 524288 | tf_op jit(solution)/shard_map/all_to_all | solution.py:21
  395.5 17.6 %all_to_all.109 = f32[32,2,256]{2,1,0:T(2,128)S(1)} all-to-all(f32[32,2,256]{2,1,0:T(2,128)S(1)} %reduce_sum.112), channel_id=1, replica_groups=mesh['col_0'=4,'col_1'=2,'row_0'=4,'row_1'=4] {'col_0','col_1','row_0'}, dimensions={0} | all-to-all | bytes 131072 | tf_op jit(solution)/shard_map/all_to_all | solution.py:29
  417.7 7.4 all-to-all-done.6
  429.4 7.2 all-to-all-done.7
  437.0 11.7 %cholesky.214 = f32[128,128]{1,0:T(8,128)S(1)} custom-call(f32[128,128]{1,0:T(8,128)S(1)} %cholesky.346), custom_call_target="Cholesky" | custom-call | tf_op jit(solution)/shard_map/jit(cholesky)/cholesky | solution.py:88
  448.7 9.8 custom-call.17
  459.0 11.7 %cholesky.231 = f32[128,128]{1,0:T(8,128)S(1)} custom-call(f32[128,128]{1,0:T(8,128)S(1)} %convolution_subtract_fusion.7), custom_call_target="Cholesky" | custom-call | tf_op jit(solution)/shard_map/jit(cholesky)/cholesky | solution.py:88
  477.7 20.1 %custom-call.18 = f32[2,128,128]{1,2,0:T(8,128)S(1)} custom-call(f32[2,128,128]{2,1,0:T(8,128)S(1)} %get-tuple-element.30), custom_call_target="InvertDiagBlocksLowerTriangular" | custom-call | tf_op jit(solution)/shard_map/jit(_solve_triangular)/triangular_solve | solution.py:89
  500.4 121.2 %all_to_all.110 = f32[16,640,256]{2,1,0:T(8,128)} all-to-all(f32[16,640,256]{2,1,0:T(8,128)S(1)} %stack.11), channel_id=1, replica_groups=mesh['col_0'=4,'col_1'=2,'row_0'=4,'row_1'=4] {'row_0','row_1'}, dimensions={0} | all-to-all | bytes 20971520 | tf_op jit(solution)/shard_map/all_to_all | solution.py:124
  621.5 13.6 %gather_fusion.1 = f32[120,128,256]{2,1,0:T(8,128)} fusion(f32[80,128,256]{2,1,0:T(8,128)} %bitcast.175, s32[1024]{0:T(1024)S(1)} %pad_clamp_fusion), kind=kCustom, calls=%fused_computation.1 | custom fusion | bytes 31457760 | tf_op jit(solution)/shard_map/gather | solution.py:135
  635.2 20.2 %convolution_bitcast_fusion.2 = f32[120,128,256]{1,2,0:T(8,128)} fusion(f32[120,128,256]{2,1,0:T(8,128)} %gather_fusion.1, bf16[120,128,128]{2,1,0:T(8,128)(2,1)} %param.8), kind=kOutput, calls=%fused_computation.14 | convolution fusion | flops 6039797760 | bytes 35389440 | tf_op jit(solution)/shard_map/sij,sjk->sik/dot_general | solution.py:136
  655.3 15.6 %copy.109 = f32[120,128,256]{2,1,0:T(8,128)} copy(f32[120,128,256]{1,2,0:T(8,128)} %convolution_bitcast_fusion.2) | data formatting | bytes 31457280 | tf_op jit(solution)/shard_map/sij,sjk->sik/dot_general | solution.py:136
  671.0 17.9 %reshape.190 = f32[120,32768,1,1]{1,0,2,3:T(8,128)} reshape(f32[120,128,256]{2,1,0:T(8,128)} %copy.109) | data formatting | bytes 31457280 | tf_op jit(solution)/shard_map/reshape | solution.py:141
  688.8 16.0 %convolution_bitcast_fusion = f32[2,4,5,32768]{3,2,0,1:T(8,128)S(1)} fusion(f32[120,32768,1,1]{1,0,2,3:T(8,128)} %reshape.190, f32[120]{0:T(128)S(1)} %copy-done.3, s32[120]{0:T(128)S(1)} %copy-done.1, s32[4,2,5]{2,1,0:T(2,128)S(1)} %multiply_add_fusion), kind=kOutput, calls=%fused_computation.10 | convolution fusion | flops 1887446400 | bytes 20972640 | tf_op jit(solution)/shard_map/dot_general | solution.py:139
  708.2 9.1 all_to_all.104
  725.3 5.3 all-to-all-start.10
  732.2 47.9 %all-to-all-done.10 = f32[4,5,32768]{2,1,0:T(8,128)} async-done(((f32[4,5,32768]{2,1,0:T(8,128)}), f32[4,5,32768]{2,1,0:T(8,128)}, u32[]{:S(2)}, u32[]{:S(2)}) %all-to-all-start.10) | async-done | bytes 2621472 | tf_op jit(solution)/shard_map/all_to_all | solution.py:29
  784.8 11.6 %all_to_all.111 = f32[4,32,1024]{2,1,0:T(8,128)S(1)} all-to-all(f32[4,32,1024]{2,1,0:T(8,128)S(1)} %maximum_bitcast_fusion), channel_id=1, replica_groups=mesh['col_0'=4,'col_1'=2,'row_0'=4,'row_1'=4] {'row_1'}, dimensions={0} | all-to-all | bytes 1048576 | tf_op jit(solution)/shard_map/all_to_all | solution.py:21
  796.5 10.9 %all_to_all.112 = f32[32,1,1024]{2,1,0:T(1,128)S(1)} all-to-all(f32[32,1,1024]{2,1,0:T(1,128)S(1)} %all_to_all.75), channel_id=1, replica_groups=mesh['col_0'=4,'col_1'=2,'row_0'=4,'row_1'=4] {'col_0','col_1','row_0'}, dimensions={0} | all-to-all | bytes 262144 | tf_op jit(solution)/shard_map/all_to_all | solution.py:29
  807.6 11.5 %all_to_all.105 = f32[32,1,1024]{2,1,0:T(1,128)S(1)} all-to-all(f32[32,1,1024]{2,1,0:T(1,128)S(1)} %broadcast_in_dim.30), channel_id=1, replica_groups=mesh['col_0'=4,'col_1'=2,'row_0'=4,'row_1'=4] {'col_0','col_1','row_0'}, dimensions={0} | all-to-all | bytes 262144 | tf_op jit(solution)/shard_map/all_to_all | solution.py:42
  823.4 10.1 all-to-all-done.14
  834.1 11.7 %cholesky.248 = f32[128,128]{1,0:T(8,128)S(1)} custom-call(f32[128,128]{1,0:T(8,128)S(1)} %cholesky.349), custom_call_target="Cholesky" | custom-call | tf_op jit(solution)/shard_map/jit(cholesky)/cholesky | solution.py:88
  845.9 9.8 custom-call.19
  856.2 11.7 %cholesky.265 = f32[128,128]{1,0:T(8,128)S(1)} custom-call(f32[128,128]{1,0:T(8,128)S(1)} %convolution_subtract_fusion.6), custom_call_target="Cholesky" | custom-call | tf_op jit(solution)/shard_map/jit(cholesky)/cholesky | solution.py:88
  874.6 19.8 %custom-call.20 = f32[2,128,128]{1,2,0:T(8,128)S(1)} custom-call(f32[2,128,128]{2,1,0:T(8,128)S(1)} %get-tuple-element.31), custom_call_target="InvertDiagBlocksLowerTriangular" | custom-call | tf_op jit(solution)/shard_map/jit(_solve_triangular)/triangular_solve | solution.py:89
  897.4 11.7 %cholesky.282 = f32[128,128]{1,0:T(8,128)S(1)} custom-call(f32[128,128]{1,0:T(8,128)S(1)} %cholesky.352), custom_call_target="Cholesky" | custom-call | tf_op jit(solution)/shard_map/jit(cholesky)/cholesky | solution.py:88
  909.2 9.8 custom-call.21
  919.5 11.9 %cholesky.299 = f32[128,128]{1,0:T(8,128)S(1)} custom-call(f32[128,128]{1,0:T(8,128)S(1)} %convolution_subtract_fusion.5), custom_call_target="Cholesky" | custom-call | tf_op jit(solution)/shard_map/jit(cholesky)/cholesky | solution.py:88
  938.1 19.7 %custom-call.22 = f32[2,128,128]{1,2,0:T(8,128)S(1)} custom-call(f32[2,128,128]{2,1,0:T(8,128)S(1)} %get-tuple-element.32), custom_call_target="InvertDiagBlocksLowerTriangular" | custom-call | tf_op jit(solution)/shard_map/jit(_solve_triangular)/triangular_solve | solution.py:89
  960.8 9.1 all_to_all.113
  970.0 10.5 all_to_all.114
  980.6 11.0 %all_to_all.106 = f32[32,2,256]{2,1,0:T(2,128)S(1)} all-to-all(f32[32,2,256]{2,1,0:T(2,128)S(1)} %broadcast_in_dim.32), channel_id=1, replica_groups=mesh['col_0'=4,'col_1'=2,'row_0'=4,'row_1'=4] {'col_0','col_1','row_0'}, dimensions={0} | all-to-all | bytes 131072 | tf_op jit(solution)/shard_map/all_to_all | solution.py:42
  997.1 6.0 all-to-all-done.18
  1003.6 11.7 %cholesky.316 = f32[128,128]{1,0:T(8,128)S(1)} custom-call(f32[128,128]{1,0:T(8,128)S(1)} %cholesky.355), custom_call_target="Cholesky" | custom-call | tf_op jit(solution)/shard_map/jit(cholesky)/cholesky | solution.py:88
  1015.3 9.8 custom-call.23
  1025.6 11.7 %cholesky.333 = f32[128,128]{1,0:T(8,128)S(1)} custom-call(f32[128,128]{1,0:T(8,128)S(1)} %convolution_subtract_fusion.4), custom_call_target="Cholesky" | custom-call | tf_op jit(solution)/shard_map/jit(cholesky)/cholesky | solution.py:88
  1044.2 20.0 %custom-call.24 = f32[2,128,128]{1,2,0:T(8,128)S(1)} custom-call(f32[2,128,128]{2,1,0:T(8,128)S(1)} %get-tuple-element.33), custom_call_target="InvertDiagBlocksLowerTriangular" | custom-call | tf_op jit(solution)/shard_map/jit(_solve_triangular)/triangular_solve | solution.py:89
  (174 shorter events, 114.2 us)
Async XLA Ops:
  1.3 279.0 %copy-start.2 = (f32[120]{0:T(128)}, f32[120]{0:T(128)S(1)}, u32[]{:S(2)}) copy-start(f32[120]{0:T(128)S(1)} %compare_convert_fusion) | copy-start | bytes 1444
  6.1 10.8 %all-to-all-start = ((f32[8,5,128]{2,1,0:T(8,128)}), f32[8,5,128]{2,1,0:T(8,128)S(1)}, u32[]{:S(2)}, u32[]{:S(2)}) async-start(f32[8,5,128]{2,1,0:T(8,128)} %fusion.51), calls=%async_computation | async-start | bytes 65536 | tf_op jit(solution)/shard_map/all_to_all | solution.py:21
  23.2 7.5 copy-start.4
  23.2 189.8 %all-to-all-start.1 = ((f32[16,640,256]{2,1,0:T(8,128)}), f32[16,640,256]{2,1,0:T(8,128)}, u32[]{:S(2)}, u32[]{:S(2)}) async-start(f32[16,640,256]{2,1,0:T(8,128)} %stack.10), calls=%async_computation.1 | async-start | bytes 20971520 | tf_op jit(solution)/shard_map/all_to_all | solution.py:124
  262.4 17.9 %copy-start.1 = (s32[120]{0:T(128)S(1)}, s32[120]{0:T(128)}, u32[]{:S(2)}) copy-start(s32[120]{0:T(128)} %param.9) | copy-start | bytes 1444
  313.4 67.5 %copy-start = (f32[640,256]{1,0:T(8,128)S(1)}, f32[640,256]{1,0:T(8,128)}, u32[]{:S(2)}) copy-start(f32[640,256]{1,0:T(8,128)} %param.12) | copy-start | bytes 1966084
  413.9 11.3 %all-to-all-start.6 = ((f32[32,2,256]{2,1,0:T(2,128)}), f32[32,2,256]{2,1,0:T(2,128)S(1)}, u32[]{:S(2)}, u32[]{:S(2)}) async-start(f32[32,2,256]{2,1,0:T(2,128)} %broadcast_in_dim.28), calls=%async_computation.6 | async-start | bytes 131072 | tf_op jit(solution)/shard_map/all_to_all | solution.py:42
  425.9 10.6 all-to-all-start.7
  477.1 0.6 copy-start.5
  671.0 17.9 %copy-start.3 = (f32[120]{0:T(128)S(1)}, f32[120]{0:T(128)}, u32[]{:S(2)}) copy-start(f32[120]{0:T(128)} %copy-done.2) | copy-start | bytes 1444
  725.3 54.7 %all-to-all-start.10 = ((f32[4,5,32768]{2,1,0:T(8,128)}), f32[4,5,32768]{2,1,0:T(8,128)}, u32[]{:S(2)}, u32[]{:S(2)}) async-start(f32[4,5,32768]{2,1,0:T(8,128)} %copy.111), calls=%async_computation.10 | async-start | bytes 8388608 | tf_op jit(solution)/shard_map/all_to_all | solution.py:29
  732.0 138.6 %copy-start.6 = (s32[2,2]{1,0:T(2,128)S(1)}, s32[2,2]{1,0:T(2,128)}, u32[]{:S(2)}) copy-start(s32[2,2]{1,0:T(2,128)} %copy-done.5) | copy-start | bytes 52
  819.9 13.6 %all-to-all-start.14 = ((f32[4,32,1024]{2,1,0:T(8,128)}), f32[4,32,1024]{2,1,0:T(8,128)S(1)}, u32[]{:S(2)}, u32[]{:S(2)}) async-start(f32[4,32,1024]{2,1,0:T(8,128)} %broadcast_in_dim.31), calls=%async_computation.14 | async-start | bytes 1048576 | tf_op jit(solution)/shard_map/all_to_all | solution.py:42
  992.3 10.8 %all-to-all-start.18 = ((f32[4,32,2,256]{3,2,1,0:T(2,128)}), f32[4,32,2,256]{3,2,1,0:T(2,128)S(1)}, u32[]{:S(2)}, u32[]{:S(2)}) async-start(f32[4,32,2,256]{3,2,1,0:T(2,128)} %broadcast_in_dim.33), calls=%async_computation.18 | async-start | bytes 524288 | tf_op jit(solution)/shard_map/all_to_all | solution.py:42
